TPU v7x, 512 devices: a whole 4x8x8 slice. The times are simulated.
512 devices in a mesh: samp: 32 (over z, x_hi, core), par: 16 (over x_lo, y).
Axes of the slice: x: 4 (x_hi: 2, x_lo: 2; x = x_hi * 2 + x_lo), y: 8, z: 8, core: 2. Of those that a mesh axis runs over, the one named last changes fastest.
Arguments:
- activations: bfloat16 [512, 2, 64, 256], P('samp'), may hold values from 0 to 2
- cotangents: bfloat16 [512, 2, 64, 256], P('samp', None, 'par'), may hold values from -0.029907227 to 0.099609375
- energies: float32 [512], P('samp'), may hold values from -3 to -1
Outputs:
- update: float32 [64, 1152], P('par')
- coeffs: float32 [512], P('samp')
All inputs are finite; a program needn't handle non-finite values.
Results may differ from a plain program's by a relative error of at most 0.0034.
Values may be sent and summed in bfloat16 or wider, within the bound.
A program may use at most 64 MiB of HBM per device.

v0:
```python
import math

import jax
import jax.numpy as jnp
from jax import lax
from jax.sharding import PartitionSpec as P

C = 64
SIDE = 16
LAYERS = 2


reg_shift = 0.1


def sample_grads(activations, cotangents):
    sample_count, layer_count, channels, site_count = activations.shape
    owned_out = cotangents.shape[2]
    field = cotangents.reshape(sample_count, layer_count, owned_out, SIDE, SIDE)
    shifted = [
        jnp.roll(field, (row_step - 1, col_step - 1), axis=(3, 4))
        for row_step in range(3)
        for col_step in range(3)
    ]
    stacked = jnp.stack(shifted, axis=3).reshape(
        sample_count, layer_count, owned_out * 9, site_count
    )
    grads = jnp.einsum("slkx,slix->slki", stacked, activations, preferred_element_type=jnp.float32)
    grads = grads.reshape(sample_count, layer_count, owned_out, 9, channels).transpose(
        0, 2, 1, 4, 3
    )
    return grads.reshape(sample_count, owned_out * layer_count * channels * 9)


def contract(left_rows, right_rows):
    return lax.dot_general(
        left_rows, right_rows, (((1,), (1,)), ((), ())), preferred_element_type=jnp.float32
    )


def solve_system(gram, dev_all, total):
    regular = gram + reg_shift * jnp.eye(total, dtype=jnp.float32)
    factor = jnp.linalg.cholesky(regular)
    forward = lax.linalg.triangular_solve(factor, dev_all[:, None], left_side=True, lower=True)
    return lax.linalg.triangular_solve(
        factor, forward, left_side=True, lower=True, transpose_a=True
    )[:, 0]


def local(activations, cotangents, energies):
    grads = sample_grads(activations, cotangents)
    local_count = grads.shape[0]
    members = lax.axis_size("samp")
    position = lax.axis_index("samp")
    total = members * local_count
    params_all = LAYERS * C * C * 9
    scale = -math.sqrt(params_all / total)
    col_sums, energy_sum = lax.psum((jnp.sum(grads, axis=0), jnp.sum(energies)), "samp")
    centered = ((grads - col_sums / total) * (1.0 / math.sqrt(params_all))).astype(jnp.bfloat16)
    deviation = energies - energy_sum / total
    partial_value = contract(centered, lax.all_gather(centered, "samp", axis=0, tiled=True))
    summed = lax.psum(partial_value, "par")
    gram, dev_column = (
        lax.all_gather(summed, "samp", axis=0, tiled=True),
        lax.all_gather(deviation[:, None], "samp", axis=0, tiled=True),
    )
    dev_all = dev_column[:, 0]
    coeffs = solve_system(gram, dev_all, total)
    local_coeffs = lax.dynamic_slice_in_dim(coeffs, position * local_count, local_count)
    term = jnp.dot(
        local_coeffs[None, :], centered.astype(jnp.float32), precision=lax.Precision.HIGHEST
    )[0]
    summed_term = lax.psum(term, "samp")
    update = scale * summed_term
    return (update.reshape(cotangents.shape[2], -1), local_coeffs)


def solution(mesh):
    return jax.shard_map(
        local,
        mesh=mesh,
        in_specs=(P("samp", None, None, None), P("samp", None, "par", None), P("samp")),
        out_specs=(P("par", None), P("samp")),
        check_vma=False,
    )
```

profile of v0, /device:TPU:1, one launch (start us, length us, event | category | flops | bytes accessed | tf_op | source)
XLA Modules:
  0.0 763.1 jit_solution(1295712559334834222)
XLA Ops:
  7.2 1.3 reshape.131
  9.5 1.0 fusion.74
  10.5 1.2 fusion.75
  11.7 1.2 fusion.72
  12.9 1.2 fusion.73
  15.0 2.5 fusion.15
  17.5 0.9 bitcast_dynamic-update-slice_fusion.2
  18.5 1.1 fusion.16
  19.6 0.6 pad_maximum_fusion.1
  20.2 0.9 fusion.20
  21.1 0.9 copy_dynamic-update-slice_fusion
  22.0 0.9 fusion.19
  22.8 1.1 fusion.17
  24.0 0.9 bitcast_dynamic-update-slice_fusion.1
  24.8 1.1 fusion.18
  25.9 6.1 reshape.132
  32.7 2.7 copy.66
  35.7 0.6 reduce_sum.22
  36.5 72.8 %psum.30 = f32[]{:T(128)} all-reduce(f32[]{:T(128)} %reduce_sum.22), channel_id=1, replica_groups=mesh['samp'=32,'par'=16] {'samp'}, use_global_device_ids=true, to_apply=%region_12.13 | all-reduce | flops 1 | bytes 8 | tf_op jit(solution)/shard_map/psum | solution.py:58
  109.3 1.3 dynamic-slice.4
  112.0 127.8 %all-reduce.2 = (f32[4608]{0:T(1024)S(1)}, f32[512]{0:T(512)S(1)}) all-reduce(f32[4608]{0:T(1024)S(1)} %reduce_sum.21, f32[512]{0:T(512)S(1)} %subtract_dynamic-update-slice_fusion), channel_id=1, replica_groups=mesh['samp'=32,'par'=16] {'samp'}, use_global_device_ids=true, to_apply=%region_1.2 | all-reduce | flops 5120 | bytes 40960 | tf_op jit(solution)/shard_map/psum | solution.py:58
  239.8 3.4 reshape.134
  243.2 0.7 multiply_convert_fusion.1
  244.0 94.5 %all-gather.4.cloned.1.call-done = bf16[512,4608]{1,0:T(8,128)(2,1)} async-done(((bf16[16,4608]{1,0:T(8,128)(2,1)}), bf16[512,4608]{1,0:T(8,128)(2,1)}) %all-gather.4.cloned.1.call-update) | async-done | bytes 4718608 | tf_op jit(solution)/shard_map/all_gather | solution.py:61
  338.5 3.7 fusion.76
  342.2 49.2 %psum.29 = f32[16,512]{1,0:T(8,128)} all-reduce(f32[16,512]{1,0:T(8,128)S(1)} %fusion.76), channel_id=1, replica_groups=mesh['samp'=32,'par'=16] {'par'}, use_global_device_ids=true, to_apply=%region_2.3 | all-reduce | flops 8192 | bytes 65536 | tf_op jit(solution)/shard_map/psum | solution.py:62
  391.9 1.1 copy.79
  393.0 2.8 convert_element_type.12
  395.9 85.4 %all-gather.6.cloned.1.call-done = f32[512,512]{1,0:T(8,128)} async-done(((f32[16,512]{1,0:T(8,128)}), f32[512,512]{1,0:T(8,128)}) %all-gather.6.cloned.1.call-update) | async-done | bytes 1048592 | tf_op jit(solution)/shard_map/all_gather | solution.py:64
  481.3 1.6 copy.68
  482.9 1.1 select_add_fusion
  484.0 1.6 copy.69
  485.8 1.0 copy-done.1
  486.8 11.7 %cholesky.103 = f32[128,128]{1,0:T(8,128)S(1)} custom-call(f32[128,128]{1,0:T(8,128)S(1)} %cholesky.263), custom_call_target="Cholesky" | custom-call | tf_op jit(solution)/shard_map/jit(cholesky)/cholesky | solution.py:43
  498.5 9.8 %custom-call.32 = f32[1,128,128]{1,2,0:T(8,128)S(1)} custom-call(f32[1,128,128]{2,1,0:T(8,128)S(1)} %get-tuple-element.55), custom_call_target="InvertDiagBlocksLowerTriangular" | custom-call | tf_op jit(solution)/shard_map/jit(cholesky)/cholesky | solution.py:43
  508.3 1.2 fusion.25
  509.6 1.3 convolution_subtract_fusion
  510.9 11.7 %cholesky.215 = f32[128,128]{1,0:T(8,128)S(1)} custom-call(f32[128,128]{1,0:T(8,128)S(1)} %cholesky.267), custom_call_target="Cholesky" | custom-call | tf_op jit(solution)/shard_map/jit(cholesky)/cholesky | solution.py:43
  523.1 10.0 %custom-call.33 = f32[1,128,128]{1,2,0:T(8,128)S(1)} custom-call(f32[1,128,128]{2,1,0:T(8,128)S(1)} %get-tuple-element.53), custom_call_target="InvertDiagBlocksLowerTriangular" | custom-call | tf_op jit(solution)/shard_map/jit(cholesky)/cholesky | solution.py:43
  533.4 1.5 convolution_subtract_fusion.1
  534.9 11.7 %cholesky.236 = f32[128,128]{1,0:T(8,128)S(1)} custom-call(f32[128,128]{1,0:T(8,128)S(1)} %cholesky.272), custom_call_target="Cholesky" | custom-call | tf_op jit(solution)/shard_map/jit(cholesky)/cholesky | solution.py:43
  546.8 9.8 %custom-call.34 = f32[1,128,128]{1,2,0:T(8,128)S(1)} custom-call(f32[1,128,128]{2,1,0:T(8,128)S(1)} %get-tuple-element.51), custom_call_target="InvertDiagBlocksLowerTriangular" | custom-call | tf_op jit(solution)/shard_map/jit(cholesky)/cholesky | solution.py:43
  556.9 1.3 convolution_subtract_fusion.2
  558.2 12.0 %cholesky.253 = f32[128,128]{1,0:T(8,128)S(1)} custom-call(f32[128,128]{1,0:T(8,128)S(1)} %convolution_subtract_fusion.2), custom_call_target="Cholesky" | custom-call | tf_op jit(solution)/shard_map/jit(cholesky)/cholesky | solution.py:43
  570.3 0.7 compare_reduce_fusion.2
  571.1 0.6 compare_reduce_fusion.3
  571.7 0.6 compare_reduce_fusion.1
  572.3 0.7 compare_reduce_fusion
  575.7 11.3 %while.1 = (s32[]{:T(128)}, f32[512,512]{0,1:T(8,128)S(1)}, s32[4,2]{0,1:T(2,128)S(1)}, f32[4,128,128]{2,1,0:T(8,128)}, s32[]{:T(128)}) while((s32[]{:T(128)}, f32[512,512]{0,1:T(8,128)S(1)}, s32[4,2]{0,1:T(2,128)S(1)}, f32[4,128,128]{2,1,0:T(8,128)}, s32[]{:T(128)}) %tuple.39), condition=%wide.while_cond, body=%wide.while_body.sunk | while | flops 2 | bytes 393829 | solution.py:45
  575.8 0.6 fusion.100
  576.4 1.4 dynamic-slice.9
  577.9 0.6 bitcast_dynamic-update-slice_fusion.4
  578.6 0.6 fusion.100
  579.2 1.4 dynamic-slice.9
  580.7 0.6 bitcast_dynamic-update-slice_fusion.4
  581.4 0.6 fusion.100
  582.0 1.4 dynamic-slice.9
  583.5 0.6 bitcast_dynamic-update-slice_fusion.4
  584.2 0.6 fusion.100
  584.8 1.4 dynamic-slice.9
  586.4 0.6 bitcast_dynamic-update-slice_fusion.4
  587.0 40.1 %custom-call.35 = f32[4,128,128]{1,2,0:T(8,128)S(1)} custom-call(f32[4,128,128]{2,1,0:T(8,128)} %get-tuple-element.9), custom_call_target="InvertDiagBlocksLowerTriangular" | custom-call | tf_op jit(solution)/shard_map/triangular_solve | solution.py:45
  630.4 124.8 %psum.31 = f32[4608]{0:T(1024)S(1)} all-reduce(f32[4608]{0:T(1024)S(1)} %convolution_reduce_fusion), channel_id=1, replica_groups=mesh['samp'=32,'par'=16] {'samp'}, use_global_device_ids=true, to_apply=%region_13.14 | all-reduce | flops 4608 | bytes 36864 | tf_op jit(solution)/shard_map/psum | solution.py:73
  755.2 0.6 reshape.144
  (89 shorter events, 9.3 us)
Async XLA Ops:
  7.2 24.9 %copy-start = (bf16[16,2,64,256]{3,2,1,0:T(8,128)(2,1)S(1)}, bf16[16,2,64,256]{3,2,1,0:T(8,128)(2,1)}, u32[]{:S(2)}) copy-start(bf16[16,2,64,256]{3,2,1,0:T(8,128)(2,1)} %param.3) | copy-start | bytes 3145732
  7.2 331.3 %all-gather.4.cloned.1.call-start = ((), (), s32[]{:S(2)}) async-start(), calls=%async_computation | async-start | bytes 4866048 | tf_op jit(solution)/shard_map/all_gather | solution.py:61
  9.5 4.6 copy-start.7
  14.5 4.0 copy-start.2
  14.5 5.1 copy-start.3
  14.5 5.1 copy-start.4
  14.5 5.1 copy-start.5
  14.5 5.1 copy-start.6
  32.0 3.7 copy-start.9
  243.9 237.4 %all-gather.6.cloned.1.call-start = ((), (), s32[]{:S(2)}) async-start(), calls=%async_computation.1 | async-start | bytes 1081344 | tf_op jit(solution)/shard_map/all_gather | solution.py:64
  485.8 1.0 copy-start.1
  630.2 125.7 %copy-start.8 = (f32[16,1]{0,1:T(1,128)}, f32[16,1]{0,1:T(1,128)S(1)}, u32[]{:S(2)}) copy-start(f32[16,1]{0,1:T(1,128)S(1)} %fusion.59) | copy-start | bytes 196
Sparse Core Ops, SparseCore 0:
  244.1 94.3 all-gather.3
  391.5 89.7 all-gather.5
where the time goes:
time: 777 us; the launch traced here: 763 us
  blocking collectives  375 us (48%)
  waiting for transfers between devices  180 us (23%)
  other arithmetic  130 us (17%)
  local copies, waits for them, and re-layouts  46.6 us (6%)
  between operations  18.8 us (2%)
  matrix products  13.2 us (2%)
    psum x2, blocking collectives, local(): lax.psum((jnp.sum(grads, axis=0), jnp.sum(energies)), 'samp')  201 us
    psum x1, blocking collectives, local(): summed_term = lax.psum(term, 'samp')  125 us
    all_gather x1, waiting for transfers between devices, local(): lax.all_gather(centered, 'samp', axis=0, tiled=True)  94.5 us
    all_gather x1, waiting for transfers between devices, local(): lax.all_gather(summed, 'samp', axis=0, tiled=True)  85.4 us
    another operation x15, other arithmetic, solve_system(): factor = jnp.linalg.cholesky(regular)  79.5 us
    psum x1, blocking collectives, local(): summed = lax.psum(partial_value, 'par')  49.2 us
    another operation x4, other arithmetic, solve_system(): lax.linalg.triangular_solve(factor, forward, left_side=True, lower=True,...  40.4 us
  transfers between devices with their start and end apart: 2, of which 2 were waited for; matrix products, arithmetic and copies ran while one was open for 1% of the time, Pallas kernels for 0%

commit v1 on v0

v1 whole, which is shorter than its diff:
```python
import math

import jax
import jax.numpy as jnp
from jax import lax
from jax.experimental import pallas as pl
from jax.experimental.pallas import tpu as pltpu
from jax.sharding import PartitionSpec as P

C = 64
SIDE = 16
LAYERS = 2
SITES = SIDE * SIDE
OFFSETS = 9

N_Z, N_XH, N_CORE = 8, 2, 2
N_SAMP = N_Z * N_XH * N_CORE
N_XL, N_Y = 2, 8
N_PAR = N_XL * N_Y
N_X = N_XH * N_XL
OWN = 16
TOTAL = N_SAMP * OWN
OUT_OWN = C // N_PAR
LANES = LAYERS * C
ROWS = OFFSETS * OUT_OWN
EXTRA = ROWS - N_SAMP
PARAMS = LAYERS * C * C * OFFSETS
REG_SHIFT = 0.1

HALF = 640
PART = HALF + 8
PLANE = N_Z * N_Y
TILES = PART // 8
FIRST = 41
FLIP = FIRST + PLANE - 1
LOW = FLIP - (TILES - 1)
SPLIT = 8 * FIRST

MESH = pl.DeviceIdType.MESH
F32 = jnp.float32
BF16 = jnp.bfloat16


def remote(src, dst, send, recv, samp, par):
    return pltpu.make_async_remote_copy(
        src_ref=src,
        dst_ref=dst,
        send_sem=send,
        recv_sem=recv,
        device_id=(samp, par),
        device_id_type=MESH,
    )


def far_first(i):
    return (4 + ((i + 1) // 2) * (1 - 2 * (i % 2))) % 8


def whole_kernel(
    act_hbm, cot_hbm, en_ref, out_ref, coeff_ref,
    act_ref, cot_ref, fields, shifted, grads, land, own, chip, part, from_plane, from_x, fin,
    rows, row_land,
    act_sem, cot_sem, a2a_send, a2a_recv, ex_send, ex_recv, core_send, core_recv, cx_send, cx_recv, r_send, r_recv, rx_send,
    p_send, p_recv, x_send, x_recv, g_send, g_recv, s_send, s_recv, rx_recv, ready,
):
    samp = lax.axis_index("samp")
    par = lax.axis_index("par")
    z = samp // 4
    x_hi = (samp // 2) % 2
    core = samp % 2
    x_lo = par // N_Y
    y = par % N_Y
    x = x_hi * 2 + x_lo
    sibling = samp + 1 - 2 * core

    act_copy = pltpu.make_async_copy(act_hbm, act_ref, act_sem)
    act_copy.start()
    cot_copy = pltpu.make_async_copy(cot_hbm, cot_ref, cot_sem)
    cot_copy.start()

    def samp_peer(i):
        to_z = (z + far_first(i // 4)) % N_Z
        to_x = (x_hi + 1 - (i // 2) % 2) % 2
        return to_z * 4 + to_x * 2 + (core + 1 - i % 2) % 2

    def plane_peer(i):
        to_z = (z + far_first(i // 8)) % N_Z
        to_y = (y + far_first(i % 8)) % N_Y
        return to_z, to_y, to_z * 4 + samp % 4, x_lo * N_Y + to_y

    def x_peer(i):
        to = (x + 3 - i) % N_X
        return z * 4 + (to // 2) * 2 + core, (to % 2) * N_Y + y

    barrier = pltpu.get_barrier_semaphore()

    def greet(to_samp, to_par):
        pl.semaphore_signal(barrier, inc=1, device_id=(to_samp, to_par), device_id_type=MESH)

    def greet_samp(i, _):
        greet(samp_peer(i), par)
        return 0

    def y_peer(i):
        return x_lo * N_Y + (y + far_first(i)) % N_Y

    def greet_y(i, _):
        greet(samp, y_peer(i))
        return 0

    lax.fori_loop(0, N_SAMP - 1, greet_samp, 0)
    lax.fori_loop(0, N_Y - 1, greet_y, 0)
    greet(*x_peer(0))
    greet(*x_peer(2))

    cot_copy.wait()
    fields[:, 0:4, :] = cot_ref[:, 0].astype(F32)
    fields[:, 4:8, :] = cot_ref[:, 1].astype(F32)
    field = fields[...].reshape(OWN * 8, SITES)
    column = lax.broadcasted_iota(jnp.int32, field.shape, 1) % SIDE
    for b in (-1, 0, 1):
        if b == 1:
            moved = jnp.where(column == 0, pltpu.roll(field, SITES - 15, 1), pltpu.roll(field, 1, 1))
        elif b == -1:
            moved = jnp.where(column == 15, pltpu.roll(field, 15, 1), pltpu.roll(field, SITES - 1, 1))
        else:
            moved = field
        for a in (-1, 0, 1):
            k = 3 * (a + 1) + (b + 1)
            turned = moved if a == 0 else pltpu.roll(moved, (16 * a) % SITES, 1)
            shifted[:, 8 * k : 8 * k + 8, :] = turned.reshape(OWN, 8, SITES)

    act_copy.wait()
    first_layer = lax.broadcasted_iota(jnp.int32, (8, LANES), 1) < C

    def one_sample(s):
        product = lax.dot_general(
            shifted[s].astype(BF16), act_ref[s], (((1,), (1,)), ((), ())), preferred_element_type=F32
        )
        for k in range(OFFSETS):
            tile = product[8 * k : 8 * k + 8, :]
            mixed = jnp.where(first_layer, tile, pltpu.roll(tile, 4, 0))
            grads[pl.ds(4 * k * OWN + s, 4, stride=OWN), :] = mixed[:4]

    def some_samples(step, _):
        for i in range(4):
            one_sample(step * 4 + i)
        return 0

    lax.fori_loop(0, OWN // 4, some_samples, 0)

    pl.semaphore_wait(barrier, N_SAMP - 1 + N_Y - 1 + 2)

    def tell_y(i, _):
        pl.semaphore_signal(ready, inc=1, device_id=(samp, y_peer(i)), device_id_type=MESH)
        return 0

    lax.fori_loop(0, N_Y - 1, tell_y, 0)

    here = pl.multiple_of(samp * OWN, OWN)

    def group(r):
        return grads.at[pl.ds(pl.multiple_of(r * OWN, OWN), OWN)]

    def send_extra(j, _):
        @pl.when(samp != 8 * j)
        def _():
            remote(group(N_SAMP + j), land.at[1, pl.ds(here, OWN)], ex_send, ex_recv, 8 * j, par).start()

        return 0

    lax.fori_loop(0, EXTRA, send_extra, 0)

    def send_group(i, _):
        to = samp_peer(i)
        remote(group(to), land.at[0, pl.ds(here, OWN)], a2a_send, a2a_recv, to, par).start()
        return 0

    lax.fori_loop(0, N_SAMP - 1, send_group, 0)
    land[0, pl.ds(here, OWN), :] = grads[pl.ds(here, OWN), :]
    is_extra = samp % 8 == 0
    chip_extra = (samp // 2) % 4 == 0

    @pl.when(is_extra)
    def _():
        mine = pl.multiple_of((N_SAMP + samp // 8) * OWN, OWN)
        land[1, pl.ds(here, OWN), :] = grads[pl.ds(mine, OWN), :]

    @pl.when(jnp.logical_not(is_extra))
    def _():
        own[1] = jnp.zeros((TOTAL, LANES), BF16)

    @pl.when(jnp.logical_not(chip_extra))
    def _():
        chip[2] = jnp.zeros((TOTAL, LANES), BF16)

    row = lax.broadcasted_iota(jnp.int32, (8, LANES), 0)
    lane = lax.broadcasted_iota(jnp.int32, (8, LANES), 1)
    own_place = (row == samp // 8) & (lane // OWN == samp % 8) & (par == 0)
    part[HALF:PART, :] = jnp.where(own_place, jnp.broadcast_to(en_ref[...], (8, LANES)), 0.0)

    def wait_recv(ref, sem):
        remote(ref, ref, a2a_send, sem, samp, par).wait_recv()

    def wait_send(ref, sem):
        remote(ref, ref, sem, a2a_recv, samp, par).wait_send()

    most = (N_SAMP - 1) * OWN

    def centre(slot):
        block = land[slot]
        mean = jnp.sum(block, axis=0, keepdims=True) / TOTAL
        return ((block - mean) * (1.0 / math.sqrt(PARAMS))).astype(BF16)

    wait_recv(land.at[0, pl.ds(0, most)], a2a_recv)
    c0 = centre(0)
    own[0] = c0
    chip[core] = c0
    remote(chip.at[core], chip.at[core], core_send, core_recv, sibling, par).start()

    @pl.when(is_extra)
    def _():
        wait_recv(land.at[1, pl.ds(0, most)], ex_recv)
        c = centre(1)
        own[1] = c
        chip[2] = c
        remote(chip.at[2], chip.at[2], cx_send, cx_recv, sibling, par).start()

    @pl.when(chip_extra & (core == 1))
    def _():
        wait_recv(chip.at[2], cx_recv)

    wait_recv(chip.at[1 - core], core_recv)

    def gram_block(i, _):
        n = core * 5 + i
        a = n % 4
        b = (a + n // 4) % 4
        total = jnp.zeros((128, 128), F32)
        for q in range(3):
            left = chip[q, pl.ds(pl.multiple_of(a * 128, 128), 128), :]
            right = chip[q, pl.ds(pl.multiple_of(b * 128, 128), 128), :]
            total += lax.dot_general(left, right, (((1,), (1,)), ((), ())), preferred_element_type=F32)
        part[pl.ds(pl.multiple_of(i * 128, 128), 128), :] = total
        return 0

    lax.fori_loop(0, 5, gram_block, 0)

    pl.semaphore_wait(ready, N_Y - 1)

    def place(at_z, at_y):
        return ((at_z * N_Y + at_y) * 13) % PLANE

    me = place(z, y)

    def tile(t):
        return pl.ds(pl.multiple_of(8 * t, 8), 8)

    def reduces(batch, q):
        return q < FIRST if batch == 0 else q >= LOW

    def tile_of(batch, q):
        return jnp.minimum(q, FIRST - 1) if batch == 0 else FLIP - jnp.maximum(q, LOW)

    def send_part(batch):
        def body(i, _):
            to_z, to_y, to_samp, to_par = plane_peer(i)
            q = place(to_z, to_y)

            @pl.when(reduces(batch, q))
            def _():
                remote(
                    part.at[tile(tile_of(batch, q))], from_plane.at[batch, me],
                    p_send.at[batch], p_recv.at[batch], to_samp, to_par,
                ).start()

            return 0

        lax.fori_loop(0, PLANE - 1, body, 0)

    def reduce_plane(batch):
        @pl.when(reduces(batch, me))
        def _():
            from_plane[batch, me] = part[tile(tile_of(batch, me)), :]
            wait_recv(from_plane.at[batch, pl.ds(0, PLANE - 1)], p_recv.at[batch])
            from_x[batch, x] = jnp.sum(from_plane[batch], axis=0)

            def send_x(i, _):
                to_samp, to_par = x_peer(i)
                mine = from_x.at[batch, x]
                remote(mine, mine, x_send.at[batch], x_recv.at[batch], to_samp, to_par).start()
                return 0

            lax.fori_loop(0, N_X - 1, send_x, 0)

    def spread_sum(batch):
        @pl.when(reduces(batch, me))
        def _():
            wait_recv(from_x.at[batch, pl.ds(0, N_X - 1)], x_recv.at[batch])
            mine = fin.at[core, tile(tile_of(batch, me))]
            fin[core, tile(tile_of(batch, me)), :] = jnp.sum(from_x[batch], axis=0)

            def send_sum(i, _):
                _, _, to_samp, to_par = plane_peer(i)
                remote(mine, mine, g_send.at[batch], g_recv.at[batch], to_samp, to_par).start()
                return 0

            lax.fori_loop(0, PLANE - 1, send_sum, 0)

    spans = ((0, SPLIT), (SPLIT, PART - SPLIT))

    def span(batch):
        start, size = spans[batch]
        return pl.ds(start, size)

    def gathered(batch):
        start, size = spans[batch]

        @pl.when(reduces(batch, me))
        def _():
            wait_recv(fin.at[core, pl.ds(start, size - 8)], g_recv.at[batch])

        @pl.when(jnp.logical_not(reduces(batch, me)))
        def _():
            wait_recv(fin.at[core, pl.ds(start, size)], g_recv.at[batch])

        remote(
            fin.at[core, span(batch)], fin.at[core, span(batch)], s_send.at[batch], s_recv.at[batch], sibling, par
        ).start()

    def complete(batch):
        wait_recv(fin.at[1 - core, span(batch)], s_recv.at[batch])

    send_part(0)
    send_part(1)
    reduce_plane(0)
    reduce_plane(1)
    spread_sum(0)
    spread_sum(1)
    gathered(0)
    complete(0)
    diag = fin[0, 0:128, :] + shift_matrix()
    first = jnp.concatenate(invert([diag[8 * q : 8 * q + 8, :] for q in range(16)]), axis=0)
    gathered(1)
    complete(1)

    solve(first, fin, own, coeff_ref, rows, samp)

    extra = N_SAMP + samp // 8

    @pl.when(is_extra)
    def _():
        def send_second(i, _):
            remote(rows.at[1, pl.ds(0, 1)], row_land.at[extra, pl.ds(0, 1)], rx_send, rx_recv.at[samp // 8], samp_peer(i), par).start()
            return 0

        lax.fori_loop(0, N_SAMP - 1, send_second, 0)
        row_land[extra] = rows[1]

    def send_row(i, _):
        remote(rows.at[0, pl.ds(0, 1)], row_land.at[samp, pl.ds(0, 1)], r_send, r_recv, samp_peer(i), par).start()
        return 0

    lax.fori_loop(0, N_SAMP - 1, send_row, 0)
    row_land[samp] = rows[0]

    wait_send(land.at[0, pl.ds(0, most)], a2a_send)

    def sent_extra(j, _):
        @pl.when(samp != 8 * j)
        def _():
            wait_send(land.at[1, pl.ds(0, OWN)], ex_send)

        return 0

    lax.fori_loop(0, EXTRA, sent_extra, 0)
    wait_send(chip.at[core], core_send)

    @pl.when(is_extra)
    def _():
        wait_send(chip.at[2], cx_send)

    for batch in range(2):

        @pl.when(reduces(batch, me))
        def _():
            wait_send(part.at[pl.ds(0, spans[batch][1] - 8)], p_send.at[batch])
            wait_send(from_x.at[batch, pl.ds(0, N_X - 1)], x_send.at[batch])
            wait_send(from_plane.at[batch, pl.ds(0, PLANE - 1)], g_send.at[batch])

        @pl.when(jnp.logical_not(reduces(batch, me)))
        def _():
            wait_send(part.at[pl.ds(0, spans[batch][1])], p_send.at[batch])

        wait_send(fin.at[core, span(batch)], s_send.at[batch])

    others = row_land.at[pl.ds(0, N_SAMP - 1), pl.ds(0, 1)]
    wait_recv(others, r_recv)

    def await_extra(j, _):
        @pl.when(samp != 8 * j)
        def _():
            wait_recv(row_land.at[0, pl.ds(0, 1)], rx_recv.at[j])

        return 0

    lax.fori_loop(0, EXTRA, await_extra, 0)
    out_ref[...] = row_land[:, 0, :]
    wait_send(others, r_send)

    @pl.when(is_extra)
    def _():
        wait_send(others, rx_send)


def whole(act, cot, energies):
    dma = pltpu.SemaphoreType.DMA
    vmem = pl.BlockSpec(memory_space=pltpu.VMEM)
    hbm = pl.BlockSpec(memory_space=pltpu.HBM)
    return pl.pallas_call(
        whole_kernel,
        out_shape=(
            jax.ShapeDtypeStruct((ROWS, LANES), F32),
            jax.ShapeDtypeStruct((1, OWN), F32),
        ),
        in_specs=[hbm, hbm, vmem],
        out_specs=(vmem, vmem),
        scratch_shapes=[
            pltpu.VMEM((OWN, LANES, SITES), BF16),
            pltpu.VMEM((OWN, LAYERS, OUT_OWN, SITES), BF16),
            pltpu.VMEM((OWN, 8, SITES), F32),
            pltpu.VMEM((OWN, 8 * OFFSETS, SITES), F32),
            pltpu.VMEM((ROWS * OWN, LANES), F32),
            pltpu.VMEM((2, TOTAL, LANES), F32),
            pltpu.VMEM((2, TOTAL, LANES), BF16),
            pltpu.VMEM((3, TOTAL, LANES), BF16),
            pltpu.VMEM((PART, LANES), F32),
            pltpu.VMEM((2, PLANE, 8, LANES), F32),
            pltpu.VMEM((2, N_X, 8, LANES), F32),
            pltpu.VMEM((N_CORE, PART, LANES), F32),
            pltpu.VMEM((2, 8, 128), F32),
            pltpu.VMEM((ROWS, 8, LANES), F32),
        ]
        + [dma] * 13
        + [dma((2,))] * 8
        + [dma((EXTRA,)), pltpu.SemaphoreType.REGULAR],
        compiler_params=pltpu.CompilerParams(
            collective_id=0, has_side_effects=True, vmem_limit_bytes=60 * 2**20
        ),
    )(act, cot, energies)


def dot(left, right, dims):
    return lax.dot_general(
        left, right, (dims, ((), ())), precision=lax.Precision.HIGHEST, preferred_element_type=F32
    )


def tree_sum(terms):
    while len(terms) > 1:
        paired = [terms[i] + terms[i + 1] for i in range(0, len(terms) - 1, 2)]
        terms = paired + terms[2 * len(paired) :]
    return terms[0]


def invert(tiles):
    tiles = list(tiles)
    lane = lax.broadcasted_iota(jnp.int32, (8, 128), 1)
    sub = lax.broadcasted_iota(jnp.int32, (8, 128), 0)
    on = [sub == r for r in range(8)]
    zero = jnp.zeros((8, 128), F32)

    def along_lanes(v, j):
        return jnp.broadcast_to(v[:, j : j + 1], (8, 128))

    def along_rows(v, j):
        return jnp.broadcast_to(v[j : j + 1, :], (8, 128))

    for p in range(8):
        base = 16 * p
        inside = (lane >= base) & (lane < base + 16)
        pivot_rows = tiles[2 * p : 2 * p + 2]
        cols = [[along_lanes(v, base + m) for m in range(16)] for v in pivot_rows]
        work = [
            jnp.where(inside, jnp.where(lane - base - 8 * t == sub, 1.0, 0.0), v) for t, v in enumerate(pivot_rows)
        ]
        for j in range(16):
            h, r = divmod(j, 8)
            inverse = 1.0 / along_rows(cols[h][j], r)

            def sweep(pair):
                turned = along_rows(pair[h], r) * inverse
                new = [pair[t] - cols[t][j] * turned for t in range(2)]
                new[h] = jnp.where(on[r], turned, new[h])
                return new

            for m in range(j + 1, 16):
                cols[0][m], cols[1][m] = sweep((cols[0][m], cols[1][m]))
            work = sweep(work)
        spread = [along_rows(work[j // 8], j % 8) for j in range(16)]
        near = [2 * p + 2, 2 * p + 3] if p < 7 else []
        rest = [q for q in range(16) if q not in near and q // 2 != p]
        new = {}
        for q in near:
            new[q] = jnp.where(inside, 0.0, tiles[q]) - tree_sum(
                [along_lanes(tiles[q], base + j) * spread[j] for j in range(16)]
            )
        left = jnp.concatenate([tiles[q] for q in rest], axis=0)
        right = jnp.concatenate([work[q - 2 * p] if q // 2 == p else zero for q in range(16)], axis=0)
        product = dot(left, right, ((1,), (0,)))
        for i, q in enumerate(rest):
            new[q] = jnp.where(inside, 0.0, tiles[q]) - product[8 * i : 8 * i + 8]
        for q in new:
            tiles[q] = new[q]
        tiles[2 * p : 2 * p + 2] = work
    return tiles


def shift_matrix():
    return jnp.where(
        lax.broadcasted_iota(jnp.int32, (128, 128), 0) == lax.broadcasted_iota(jnp.int32, (128, 128), 1),
        REG_SHIFT, 0.0,
    ).astype(F32)


def solve(first, fin, own, coeff_ref, rows, samp):
    B = 128
    blocks = {}
    for n in range(10):
        a = n % 4
        b = (a + n // 4) % 4
        core, i = divmod(n, 5)
        value = fin[core, B * i : B * i + B, :]
        if a == b:
            value = value + shift_matrix()
        if a > b:
            a, b, value = b, a, value.T
        blocks[a, b] = value

    energies = fin[0, HALF:PART, :] + fin[1, HALF:PART, :]
    mean = jnp.sum(energies, axis=(0, 1), keepdims=True) / TOTAL
    rhs = [jnp.broadcast_to(energies[a : a + 1, :] - mean, (8, B)) for a in range(4)]

    upper = {}
    for s in range(4):
        if s == 0:
            p = first
        else:
            p = jnp.concatenate(invert([blocks[s, s][8 * q : 8 * q + 8] for q in range(16)]), axis=0)
        for j in range(s + 1, 4):
            upper[s, j] = dot(p, blocks[s, j], ((1,), (0,)))
        for i in range(s + 1, 4):
            for j in range(i, 4):
                blocks[i, j] = blocks[i, j] - dot(blocks[s, i], upper[s, j], ((0,), (0,)))
        u = dot(rhs[s], p, ((1,), (0,)))
        for j in range(s + 1, 4):
            rhs[j] = rhs[j] - dot(u, blocks[s, j], ((1,), (0,)))
        rhs[s] = u
    for s in (2, 1, 0):
        for j in range(s + 1, 4):
            rhs[s] = rhs[s] - dot(rhs[j], upper[s, j], ((1,), (1,)))

    scale = -math.sqrt(PARAMS / TOTAL)
    mine = rhs[0]
    for a in range(1, 4):
        mine = jnp.where(samp // 8 == a, rhs[a], mine)
    coeff_ref[...] = pltpu.roll(mine, (128 - OWN * (samp % 8)) % 128, 1)[0:1, 0:OWN]
    for slot in range(2):
        total = jnp.zeros((8, B), F32)
        for a in range(4):
            total += dot(rhs[a], own[slot, B * a : B * a + B, :].astype(F32), ((1,), (0,)))
        rows[slot] = scale * total


def local(activations, cotangents, energies):
    act = activations.reshape(OWN, LANES, SITES)
    spread = jnp.tile(energies, 128 // OWN).reshape(1, LANES)
    rows, coeffs = whole(act, cotangents, spread)
    update = rows.reshape(OFFSETS, OUT_OWN, LANES).transpose(1, 2, 0).reshape(OUT_OWN, -1)
    return update, coeffs.reshape(OWN)


def solution(mesh):
    return jax.shard_map(
        local,
        mesh=mesh,
        in_specs=(P("samp", None, None, None), P("samp", None, "par", None), P("samp")),
        out_specs=(P("par", None), P("samp")),
        check_vma=False,
    )
```

time: 777 us -> 80.7 us (0.10); the launches traced: 763 us -> 79.8 us
  blocking collectives: 375 us -> 0 us
  waiting for transfers between devices: 180 us -> 0 us
  other arithmetic: 130 us -> 0 us
  Pallas kernels: 0 us -> 75.7 us
  local copies, waits for them, and re-layouts: 46.6 us -> 3.45 us
  between operations: 18.8 us -> 0.66 us
  matrix products: 13.2 us -> 0 us
    psum x4 -> x0, blocking collectives: 375 us -> none  [the longest x2 201 us: local(): lax.psum((jnp.sum(grads, axis=0), jnp.sum(energies)), 'samp')]
    all_gather x2 -> x0, waiting for transfers between devices: 180 us -> none  [the longest x1 94.5 us: local(): lax.all_gather(centered, 'samp', axis=0, tiled=True)]
    another operation x20 -> x0, other arithmetic: 121 us -> none  [the longest x15 79.5 us: solve_system(): factor = jnp.linalg.cholesky(regular)]
    pallas_call x0 -> x1, Pallas kernels: none -> 75.7 us  [whole(): pl.pallas_call(whole_kernel, out_shape=(jax.ShapeDtypeStruct((ROWS, LANES...]
    another operation x35 -> x2, local copies, waits for them, and re-layouts: 12.3 us -> 0.6 us  [local(): spread = jnp.tile(energies, 128 // OWN).reshape(1, LANES)]
    reshape x4 -> x3, local copies, waits for them, and re-layouts: 11.4 us -> 1.7 us  [local(): rows.reshape(OFFSETS, OUT_OWN, LANES).transpose(1, 2, 0)]
    another operation x20 -> x0, matrix products: 8.83 us -> none  [the longest x6 5.92 us: solve_system(): factor = jnp.linalg.cholesky(regular)]
  transfers between devices with their start and end apart: 2 -> 0, of which waited for: 2 -> 0; matrix products, arithmetic and copies ran while one was open for 1% -> 0% of each run, Pallas kernels for 0% -> 0%
where the time goes in v1:
time: 80.7 us; the launch traced here: 79.8 us
  Pallas kernels  75.7 us (94%)
  local copies, waits for them, and re-layouts  3.45 us (4%)
    pallas_call x1, Pallas kernels, whole(): pl.pallas_call(whole_kernel, out_shape=(jax.ShapeDtypeStruct((ROWS, LANES...  75.7 us
    reshape x3, local copies, waits for them, and re-layouts, local(): rows.reshape(OFFSETS, OUT_OWN, LANES).transpose(1, 2, 0)  1.7 us

profile of v1, /device:TPU:1, one launch (start us, length us, event | category | flops | bytes accessed | tf_op | source)
XLA Modules:
  0.0 79.8 jit_solution(9266642483163111484)
XLA Ops:
  0.6 0.0 copy-start
  0.6 0.6 copy-done
  1.3 0.6 reshape_tile.3.en_ref
  1.9 75.7 %shard_map.50 = (f32[36,128]{1,0:T(8,128)}, f32[1,16]{1,0:T(1,128)}) custom-call(bf16[16,128,256]{2,1,0:T(8,128)(2,1)} %bitcast.3, bf16[16,2,4,256]{3,2,1,0:T(4,128)(2,1)} %cot_hbm.1, f32[1,128]{1,0:T(1,128)} %reshape_tile.3.en_ref), custom_call_target="tpu_custom_call" | custom-call | tf_op jit(solution)/shard_map/pallas_call | solution.py:420
  77.6 0.7 reshape.18
  78.3 0.1 copy.6
  78.5 0.0 copy-start.1
  78.5 0.8 %reshape.19 = f32[4,1152]{1,0:T(4,128)} reshape(f32[4,128,9]{2,1,0:T(8,128)S(1)} %bitcast.4) | data formatting | bytes 36864 | tf_op jit(solution)/shard_map/reshape | solution.py:579
  79.3 0.0 copy-done.1
  79.3 0.5 copy.8
  (1 shorter events, 0.0 us)
Async XLA Ops:
  0.6 0.7 copy-start
  78.5 0.8 %copy-start.1 = (f32[1,16]{1,0:T(1,128)S(1)}, f32[1,16]{1,0:T(1,128)}, u32[]{:S(2)}) copy-start(f32[1,16]{1,0:T(1,128)} %get-tuple-element.5) | copy-start | bytes 196

commit v2 on v1

--- a/solution.py
+++ b/solution.py
@@ -57,10 +57,10 @@
 
 
 def whole_kernel(
-    act_hbm, cot_hbm, en_ref, out_ref, coeff_ref,
-    act_ref, cot_ref, fields, shifted, grads, land, own, chip, part, from_plane, from_x, fin,
+    act_hbm, cot_hbm, en_hbm, out_ref, coeff_ref,
+    act_ref, cot_ref, en_ref, spot, fields, shifted, grads, land, own, chip, part, from_plane, from_x, fin,
     rows, row_land,
-    act_sem, cot_sem, a2a_send, a2a_recv, ex_send, ex_recv, core_send, core_recv, cx_send, cx_recv, r_send, r_recv, rx_send,
+    act_sem, cot_sem, en_sem, a2a_send, a2a_recv, ex_send, ex_recv, core_send, core_recv, cx_send, cx_recv, r_send, r_recv, rx_send,
     p_send, p_recv, x_send, x_recv, g_send, g_recv, s_send, s_recv, rx_recv, ready,
 ):
     samp = lax.axis_index("samp")
@@ -77,6 +77,8 @@
     act_copy.start()
     cot_copy = pltpu.make_async_copy(cot_hbm, cot_ref, cot_sem)
     cot_copy.start()
+    en_copy = pltpu.make_async_copy(en_hbm, en_ref, en_sem)
+    en_copy.start()
 
     def samp_peer(i):
         to_z = (z + far_first(i // 4)) % N_Z
@@ -131,24 +133,54 @@
             shifted[:, 8 * k : 8 * k + 8, :] = turned.reshape(OWN, 8, SITES)
 
     act_copy.wait()
+    en_copy.wait()
     first_layer = lax.broadcasted_iota(jnp.int32, (8, LANES), 1) < C
 
-    def one_sample(s):
+    half = OWN // 2
+
+    def one_sample(part_no, i):
+        s = part_no * half + i
         product = lax.dot_general(
             shifted[s].astype(BF16), act_ref[s], (((1,), (1,)), ((), ())), preferred_element_type=F32
         )
         for k in range(OFFSETS):
             tile = product[8 * k : 8 * k + 8, :]
             mixed = jnp.where(first_layer, tile, pltpu.roll(tile, 4, 0))
-            grads[pl.ds(4 * k * OWN + s, 4, stride=OWN), :] = mixed[:4]
-
-    def some_samples(step, _):
-        for i in range(4):
-            one_sample(step * 4 + i)
-        return 0
-
-    lax.fori_loop(0, OWN // 4, some_samples, 0)
-
+            grads[part_no, pl.ds(4 * k * half + i, 4, stride=half), :] = mixed[:4]
+
+    def some_samples(part_no):
+        def body(step, _):
+            for i in range(4):
+                one_sample(part_no, step * 4 + i)
+            return 0
+
+        lax.fori_loop(0, half // 4, body, 0)
+
+    here = pl.multiple_of(samp * OWN, OWN)
+
+    def send_groups(part_no):
+        there = pl.ds(pl.multiple_of(here + part_no * half, half), half)
+
+        def group(r):
+            return grads.at[part_no, pl.ds(pl.multiple_of(r * half, half), half)]
+
+        def send_extra(j, _):
+            @pl.when(samp != 8 * j)
+            def _():
+                remote(group(N_SAMP + j), land.at[1, there], ex_send, ex_recv, 8 * j, par).start()
+
+            return 0
+
+        lax.fori_loop(0, EXTRA, send_extra, 0)
+
+        def send_group(i, _):
+            to = samp_peer(i)
+            remote(group(to), land.at[0, there], a2a_send, a2a_recv, to, par).start()
+            return 0
+
+        lax.fori_loop(0, N_SAMP - 1, send_group, 0)
+
+    some_samples(0)
     pl.semaphore_wait(barrier, N_SAMP - 1 + N_Y - 1 + 2)
 
     def tell_y(i, _):
@@ -157,34 +189,22 @@
 
     lax.fori_loop(0, N_Y - 1, tell_y, 0)
 
-    here = pl.multiple_of(samp * OWN, OWN)
-
-    def group(r):
-        return grads.at[pl.ds(pl.multiple_of(r * OWN, OWN), OWN)]
-
-    def send_extra(j, _):
-        @pl.when(samp != 8 * j)
-        def _():
-            remote(group(N_SAMP + j), land.at[1, pl.ds(here, OWN)], ex_send, ex_recv, 8 * j, par).start()
-
-        return 0
-
-    lax.fori_loop(0, EXTRA, send_extra, 0)
-
-    def send_group(i, _):
-        to = samp_peer(i)
-        remote(group(to), land.at[0, pl.ds(here, OWN)], a2a_send, a2a_recv, to, par).start()
-        return 0
-
-    lax.fori_loop(0, N_SAMP - 1, send_group, 0)
-    land[0, pl.ds(here, OWN), :] = grads[pl.ds(here, OWN), :]
+    send_groups(0)
+    some_samples(1)
+    send_groups(1)
+
+    def keep(slot, r):
+        for part_no in range(2):
+            there = pl.ds(pl.multiple_of(here + part_no * half, half), half)
+            land[slot, there, :] = grads[part_no, pl.ds(pl.multiple_of(r * half, half), half), :]
+
+    keep(0, samp)
     is_extra = samp % 8 == 0
     chip_extra = (samp // 2) % 4 == 0
 
     @pl.when(is_extra)
     def _():
-        mine = pl.multiple_of((N_SAMP + samp // 8) * OWN, OWN)
-        land[1, pl.ds(here, OWN), :] = grads[pl.ds(mine, OWN), :]
+        keep(1, N_SAMP + samp // 8)
 
     @pl.when(jnp.logical_not(is_extra))
     def _():
@@ -197,7 +217,10 @@
     row = lax.broadcasted_iota(jnp.int32, (8, LANES), 0)
     lane = lax.broadcasted_iota(jnp.int32, (8, LANES), 1)
     own_place = (row == samp // 8) & (lane // OWN == samp % 8) & (par == 0)
-    part[HALF:PART, :] = jnp.where(own_place, jnp.broadcast_to(en_ref[...], (8, LANES)), 0.0)
+    spot[...] = jnp.zeros((8, LANES), F32)
+    spot[0:1, 0:OWN] = en_ref[...]
+    moved = pltpu.roll(spot[...], OWN * (samp % 8), 1)
+    part[HALF:PART, :] = jnp.where(own_place, jnp.broadcast_to(moved[0:1, :], (8, LANES)), 0.0)
 
     def wait_recv(ref, sem):
         remote(ref, ref, a2a_send, sem, samp, par).wait_recv()
@@ -211,6 +234,14 @@
         block = land[slot]
         mean = jnp.sum(block, axis=0, keepdims=True) / TOTAL
         return ((block - mean) * (1.0 / math.sqrt(PARAMS))).astype(BF16)
+
+    @pl.when(is_extra)
+    def _():
+        wait_recv(land.at[1, pl.ds(0, most)], ex_recv)
+        c = centre(1)
+        own[1] = c
+        chip[2] = c
+        remote(chip.at[2], chip.at[2], cx_send, cx_recv, sibling, par).start()
 
     wait_recv(land.at[0, pl.ds(0, most)], a2a_recv)
     c0 = centre(0)
@@ -218,21 +249,13 @@
     chip[core] = c0
     remote(chip.at[core], chip.at[core], core_send, core_recv, sibling, par).start()
 
-    @pl.when(is_extra)
-    def _():
-        wait_recv(land.at[1, pl.ds(0, most)], ex_recv)
-        c = centre(1)
-        own[1] = c
-        chip[2] = c
-        remote(chip.at[2], chip.at[2], cx_send, cx_recv, sibling, par).start()
-
     @pl.when(chip_extra & (core == 1))
     def _():
         wait_recv(chip.at[2], cx_recv)
 
     wait_recv(chip.at[1 - core], core_recv)
 
-    def gram_block(i, _):
+    def gram_block(i):
         n = core * 5 + i
         a = n % 4
         b = (a + n // 4) % 4
@@ -241,10 +264,7 @@
             left = chip[q, pl.ds(pl.multiple_of(a * 128, 128), 128), :]
             right = chip[q, pl.ds(pl.multiple_of(b * 128, 128), 128), :]
             total += lax.dot_general(left, right, (((1,), (1,)), ((), ())), preferred_element_type=F32)
-        part[pl.ds(pl.multiple_of(i * 128, 128), 128), :] = total
-        return 0
-
-    lax.fori_loop(0, 5, gram_block, 0)
+        part[128 * i : 128 * i + 128, :] = total
 
     pl.semaphore_wait(ready, N_Y - 1)
 
@@ -331,7 +351,11 @@
     def complete(batch):
         wait_recv(fin.at[1 - core, span(batch)], s_recv.at[batch])
 
+    for i in range(3):
+        gram_block(i)
     send_part(0)
+    for i in range(3, 5):
+        gram_block(i)
     send_part(1)
     reduce_plane(0)
     reduce_plane(1)
@@ -405,7 +429,10 @@
         return 0
 
     lax.fori_loop(0, EXTRA, await_extra, 0)
-    out_ref[...] = row_land[:, 0, :]
+    for o in range(OUT_OWN):
+        taken = [row_land[k * OUT_OWN + o, 0:1, :] for k in range(OFFSETS)]
+        taken.append(jnp.zeros((16 - OFFSETS, LANES), F32))
+        out_ref[o] = jnp.concatenate(taken, axis=0).T[:, 0:OFFSETS]
     wait_send(others, r_send)
 
     @pl.when(is_extra)
@@ -420,17 +447,19 @@
     return pl.pallas_call(
         whole_kernel,
         out_shape=(
-            jax.ShapeDtypeStruct((ROWS, LANES), F32),
+            jax.ShapeDtypeStruct((OUT_OWN, LANES, OFFSETS), F32),
             jax.ShapeDtypeStruct((1, OWN), F32),
         ),
-        in_specs=[hbm, hbm, vmem],
+        in_specs=[hbm, hbm, hbm],
         out_specs=(vmem, vmem),
         scratch_shapes=[
             pltpu.VMEM((OWN, LANES, SITES), BF16),
             pltpu.VMEM((OWN, LAYERS, OUT_OWN, SITES), BF16),
+            pltpu.VMEM((1, OWN), F32),
+            pltpu.VMEM((8, LANES), F32),
             pltpu.VMEM((OWN, 8, SITES), F32),
             pltpu.VMEM((OWN, 8 * OFFSETS, SITES), F32),
-            pltpu.VMEM((ROWS * OWN, LANES), F32),
+            pltpu.VMEM((2, ROWS * OWN // 2, LANES), F32),
             pltpu.VMEM((2, TOTAL, LANES), F32),
             pltpu.VMEM((2, TOTAL, LANES), BF16),
             pltpu.VMEM((3, TOTAL, LANES), BF16),
@@ -441,7 +470,7 @@
             pltpu.VMEM((2, 8, 128), F32),
             pltpu.VMEM((ROWS, 8, LANES), F32),
         ]
-        + [dma] * 13
+        + [dma] * 14
         + [dma((2,))] * 8
         + [dma((EXTRA,)), pltpu.SemaphoreType.REGULAR],
         compiler_params=pltpu.CompilerParams(
@@ -542,6 +571,7 @@
     rhs = [jnp.broadcast_to(energies[a : a + 1, :] - mean, (8, B)) for a in range(4)]
 
     upper = {}
+    sol = {}
     for s in range(4):
         if s == 0:
             p = first
@@ -549,34 +579,35 @@
             p = jnp.concatenate(invert([blocks[s, s][8 * q : 8 * q + 8] for q in range(16)]), axis=0)
         for j in range(s + 1, 4):
             upper[s, j] = dot(p, blocks[s, j], ((1,), (0,)))
-        for i in range(s + 1, 4):
-            for j in range(i, 4):
+            for i in range(s + 1, j + 1):
                 blocks[i, j] = blocks[i, j] - dot(blocks[s, i], upper[s, j], ((0,), (0,)))
-        u = dot(rhs[s], p, ((1,), (0,)))
+        sol[s] = dot(rhs[s], p, ((1,), (0,)))
         for j in range(s + 1, 4):
-            rhs[j] = rhs[j] - dot(u, blocks[s, j], ((1,), (0,)))
-        rhs[s] = u
-    for s in (2, 1, 0):
-        for j in range(s + 1, 4):
-            rhs[s] = rhs[s] - dot(rhs[j], upper[s, j], ((1,), (1,)))
+            rhs[j] = rhs[j] - dot(sol[s], blocks[s, j], ((1,), (0,)))
+        for i in range(s):
+            sol[i] = sol[i] - dot(sol[s], upper[i, s], ((1,), (1,)))
+            for j in range(s + 1, 4):
+                upper[i, j] = upper[i, j] - dot(upper[i, s], upper[s, j], ((1,), (0,)))
 
     scale = -math.sqrt(PARAMS / TOTAL)
-    mine = rhs[0]
+    mine = sol[0]
     for a in range(1, 4):
-        mine = jnp.where(samp // 8 == a, rhs[a], mine)
+        mine = jnp.where(samp // 8 == a, sol[a], mine)
     coeff_ref[...] = pltpu.roll(mine, (128 - OWN * (samp % 8)) % 128, 1)[0:1, 0:OWN]
+    coeffs = jnp.concatenate([sol[a] for a in range(4)], axis=1)
+    high = coeffs.astype(BF16).astype(F32)
+    middle = (coeffs - high).astype(BF16).astype(F32)
+    low = coeffs - high - middle
+    terms = jnp.concatenate([high, middle, low, jnp.zeros((8, TOTAL), F32)], axis=0).astype(BF16)
     for slot in range(2):
-        total = jnp.zeros((8, B), F32)
-        for a in range(4):
-            total += dot(rhs[a], own[slot, B * a : B * a + B, :].astype(F32), ((1,), (0,)))
-        rows[slot] = scale * total
+        total = lax.dot_general(terms, own[slot], (((1,), (0,)), ((), ())), preferred_element_type=F32)
+        rows[slot] = scale * (total[0:8] + (total[8:16] + total[16:24]))
 
 
 def local(activations, cotangents, energies):
     act = activations.reshape(OWN, LANES, SITES)
-    spread = jnp.tile(energies, 128 // OWN).reshape(1, LANES)
-    rows, coeffs = whole(act, cotangents, spread)
-    update = rows.reshape(OFFSETS, OUT_OWN, LANES).transpose(1, 2, 0).reshape(OUT_OWN, -1)
+    rows, coeffs = whole(act, cotangents, energies.reshape(1, OWN))
+    update = rows.reshape(OUT_OWN, -1)
     return update, coeffs.reshape(OWN)
 
 

time: 80.7 us -> 79.1 us (0.980)
    reshape x3 -> x1, local copies, waits for them, and re-layouts: 1.7 us -> 1.77 us  [local(): update = rows.reshape(OUT_OWN, -1)]
where the time goes in v2:
time: 79.1 us; the launch traced here: 78.9 us
  Pallas kernels  75.4 us (95%)
  local copies, waits for them, and re-layouts  2.85 us (4%)
    pallas_call x1, Pallas kernels, whole(): pl.pallas_call(whole_kernel, out_shape=(jax.ShapeDtypeStruct((OUT_OWN, LA...  75.4 us
    reshape x1, local copies, waits for them, and re-layouts, local(): update = rows.reshape(OUT_OWN, -1)  1.77 us

profile of v2, /device:TPU:1, one launch (start us, length us, event | category | flops | bytes accessed | tf_op | source)
XLA Modules:
  0.0 78.9 jit_solution(2902103586523048235)
XLA Ops:
  0.6 75.4 %shard_map.50 = (f32[4,128,9]{2,1,0:T(8,128)}, f32[1,16]{1,0:T(1,128)}) custom-call(bf16[16,128,256]{2,1,0:T(8,128)(2,1)} %bitcast.3, bf16[16,2,4,256]{3,2,1,0:T(4,128)(2,1)} %cot_hbm.1, f32[1,16]{1,0:T(1,128)} %bitcast.4), custom_call_target="tpu_custom_call" | custom-call | tf_op jit(solution)/shard_map/pallas_call | solution.py:447
  76.0 1.8 %reshape.18 = f32[4,1152]{1,0:T(4,128)} reshape(f32[4,128,9]{2,1,0:T(8,128)} %get-tuple-element.4) | data formatting | bytes 36864 | tf_op jit(solution)/shard_map/reshape | solution.py:610
  77.8 0.0 copy-start
  77.8 0.6 copy-done
  78.4 0.5 copy.6
Async XLA Ops:
  77.8 0.6 copy-start

commit v3 on v2

--- a/solution.py
+++ b/solution.py
@@ -31,10 +31,14 @@
 PART = HALF + 8
 PLANE = N_Z * N_Y
 TILES = PART // 8
-FIRST = 41
+FIRST = 24
 FLIP = FIRST + PLANE - 1
 LOW = FLIP - (TILES - 1)
 SPLIT = 8 * FIRST
+PIECES = (
+    ((0, 0, 0), (0, 0, 1), (0, 1, 0), (0, 2, 0), (0, 2, 1), (0, 3, 0), (0, 3, 1), (1, 2, 0), (1, 2, 1), (1, 3, 0)),
+    ((1, 1, 0), (1, 1, 1), (0, 1, 1), (1, 3, 1), (2, 2, 0), (2, 2, 1), (2, 3, 0), (2, 3, 1), (3, 3, 0), (3, 3, 1)),
+)
 
 MESH = pl.DeviceIdType.MESH
 F32 = jnp.float32
@@ -255,16 +259,17 @@
 
     wait_recv(chip.at[1 - core], core_recv)
 
-    def gram_block(i):
-        n = core * 5 + i
-        a = n % 4
-        b = (a + n // 4) % 4
-        total = jnp.zeros((128, 128), F32)
+    def gram_piece(i):
+        (a0, b0, h0), (a1, b1, h1) = PIECES[0][i], PIECES[1][i]
+        left0, left1 = 128 * a0 + 64 * h0, 128 * a1 + 64 * h1
+        left_row = pl.multiple_of(left0 + core * (left1 - left0), 64)
+        right_row = pl.multiple_of(128 * (b0 + core * (b1 - b0)), 128)
+        total = jnp.zeros((64, 128), F32)
         for q in range(3):
-            left = chip[q, pl.ds(pl.multiple_of(a * 128, 128), 128), :]
-            right = chip[q, pl.ds(pl.multiple_of(b * 128, 128), 128), :]
+            left = chip[q, pl.ds(left_row, 64), :]
+            right = chip[q, pl.ds(right_row, 128), :]
             total += lax.dot_general(left, right, (((1,), (1,)), ((), ())), preferred_element_type=F32)
-        part[128 * i : 128 * i + 128, :] = total
+        part[64 * i : 64 * i + 64, :] = total
 
     pl.semaphore_wait(ready, N_Y - 1)
 
@@ -352,10 +357,10 @@
         wait_recv(fin.at[1 - core, span(batch)], s_recv.at[batch])
 
     for i in range(3):
-        gram_block(i)
+        gram_piece(i)
     send_part(0)
-    for i in range(3, 5):
-        gram_block(i)
+    for i in range(3, 10):
+        gram_piece(i)
     send_part(1)
     reduce_plane(0)
     reduce_plane(1)
@@ -363,12 +368,15 @@
     spread_sum(1)
     gathered(0)
     complete(0)
-    diag = fin[0, 0:128, :] + shift_matrix()
-    first = jnp.concatenate(invert([diag[8 * q : 8 * q + 8, :] for q in range(16)]), axis=0)
+    first = join(invert(split(gram_block(fin, 0, 0))))
+    across = gram_block(fin, 0, 1)
+    above = dot(first, across, ((1,), (0,)))
+    second = invert(split(gram_block(fin, 1, 1) - dot(across, above, ((0,), (0,)))), range(4))
     gathered(1)
+    second = join(invert(second, range(4, 8)))
     complete(1)
 
-    solve(first, fin, own, coeff_ref, rows, samp)
+    solve(first, above, second, fin, own, coeff_ref, rows, samp)
 
     extra = N_SAMP + samp // 8
 
@@ -429,10 +437,9 @@
         return 0
 
     lax.fori_loop(0, EXTRA, await_extra, 0)
-    for o in range(OUT_OWN):
-        taken = [row_land[k * OUT_OWN + o, 0:1, :] for k in range(OFFSETS)]
-        taken.append(jnp.zeros((16 - OFFSETS, LANES), F32))
-        out_ref[o] = jnp.concatenate(taken, axis=0).T[:, 0:OFFSETS]
+    for k in range(OFFSETS):
+        for o in range(OUT_OWN):
+            out_ref[o, k : k + 1, :] = row_land[k * OUT_OWN + o, 0:1, :]
     wait_send(others, r_send)
 
     @pl.when(is_extra)
@@ -447,7 +454,7 @@
     return pl.pallas_call(
         whole_kernel,
         out_shape=(
-            jax.ShapeDtypeStruct((OUT_OWN, LANES, OFFSETS), F32),
+            jax.ShapeDtypeStruct((OUT_OWN, OFFSETS, LANES), F32),
             jax.ShapeDtypeStruct((1, OWN), F32),
         ),
         in_specs=[hbm, hbm, hbm],
@@ -492,7 +499,25 @@
     return terms[0]
 
 
-def invert(tiles):
+def gram_block(fin, a, b):
+    halves = []
+    for h in range(2):
+        core = 0 if (a, b, h) in PIECES[0] else 1
+        i = PIECES[core].index((a, b, h))
+        halves.append(fin[core, 64 * i : 64 * i + 64, :])
+    value = jnp.concatenate(halves, axis=0)
+    return value + shift_matrix() if a == b else value
+
+
+def split(matrix):
+    return [matrix[8 * q : 8 * q + 8] for q in range(16)]
+
+
+def join(tiles):
+    return jnp.concatenate(tiles, axis=0)
+
+
+def invert(tiles, panels=range(8)):
     tiles = list(tiles)
     lane = lax.broadcasted_iota(jnp.int32, (8, 128), 1)
     sub = lax.broadcasted_iota(jnp.int32, (8, 128), 0)
@@ -505,7 +530,7 @@
     def along_rows(v, j):
         return jnp.broadcast_to(v[j : j + 1, :], (8, 128))
 
-    for p in range(8):
+    for p in panels:
         base = 16 * p
         inside = (lane >= base) & (lane < base + 16)
         pivot_rows = tiles[2 * p : 2 * p + 2]
@@ -552,19 +577,9 @@
     ).astype(F32)
 
 
-def solve(first, fin, own, coeff_ref, rows, samp):
+def solve(first, above, second, fin, own, coeff_ref, rows, samp):
     B = 128
-    blocks = {}
-    for n in range(10):
-        a = n % 4
-        b = (a + n // 4) % 4
-        core, i = divmod(n, 5)
-        value = fin[core, B * i : B * i + B, :]
-        if a == b:
-            value = value + shift_matrix()
-        if a > b:
-            a, b, value = b, a, value.T
-        blocks[a, b] = value
+    blocks = {(a, b): gram_block(fin, a, b) for a in range(4) for b in range(a, 4)}
 
     energies = fin[0, HALF:PART, :] + fin[1, HALF:PART, :]
     mean = jnp.sum(energies, axis=(0, 1), keepdims=True) / TOTAL
@@ -573,13 +588,12 @@
     upper = {}
     sol = {}
     for s in range(4):
-        if s == 0:
-            p = first
-        else:
-            p = jnp.concatenate(invert([blocks[s, s][8 * q : 8 * q + 8] for q in range(16)]), axis=0)
+        p = (first, second)[s] if s < 2 else join(invert(split(blocks[s, s])))
         for j in range(s + 1, 4):
-            upper[s, j] = dot(p, blocks[s, j], ((1,), (0,)))
+            upper[s, j] = above if (s, j) == (0, 1) else dot(p, blocks[s, j], ((1,), (0,)))
             for i in range(s + 1, j + 1):
+                if (s, i, j) == (0, 1, 1):
+                    continue
                 blocks[i, j] = blocks[i, j] - dot(blocks[s, i], upper[s, j], ((0,), (0,)))
         sol[s] = dot(rhs[s], p, ((1,), (0,)))
         for j in range(s + 1, 4):
@@ -607,7 +621,7 @@
 def local(activations, cotangents, energies):
     act = activations.reshape(OWN, LANES, SITES)
     rows, coeffs = whole(act, cotangents, energies.reshape(1, OWN))
-    update = rows.reshape(OUT_OWN, -1)
+    update = rows.transpose(0, 2, 1).reshape(OUT_OWN, -1)
     return update, coeffs.reshape(OWN)
 
 

time: 79.1 us -> 78.8 us (level)
    reshape x1, local copies, waits for them, and re-layouts: 1.77 us -> 0.82 us  [local(): update = rows.transpose(0, 2, 1).reshape(OUT_OWN, -1)]
    transpose x0 -> x1, local copies, waits for them, and re-layouts: none -> 0.89 us  [local(): update = rows.transpose(0, 2, 1).reshape(OUT_OWN, -1)]
where the time goes in v3:
time: 78.8 us; the launch traced here: 78.6 us
  Pallas kernels  75.7 us (96%)
  local copies, waits for them, and re-layouts  2.22 us (3%)
    pallas_call x1, Pallas kernels, whole(): pl.pallas_call(whole_kernel, out_shape=(jax.ShapeDtypeStruct((OUT_OWN, OF...  75.7 us

profile of v3, /device:TPU:1, one launch (start us, length us, event | category | flops | bytes accessed | tf_op | source)
XLA Modules:
  0.0 78.6 jit_solution(11390264834971840837)
XLA Ops:
  0.6 75.7 %shard_map.50 = (f32[4,9,128]{2,1,0:T(8,128)}, f32[1,16]{1,0:T(1,128)}) custom-call(bf16[16,128,256]{2,1,0:T(8,128)(2,1)} %bitcast.4, bf16[16,2,4,256]{3,2,1,0:T(4,128)(2,1)} %cot_hbm.1, f32[1,16]{1,0:T(1,128)} %bitcast.6), custom_call_target="tpu_custom_call" | custom-call | tf_op jit(solution)/shard_map/pallas_call | solution.py:454
  76.3 0.9 %copy.5 = f32[4,128,9]{2,1,0:T(8,128)S(1)} copy(f32[4,128,9]{1,2,0:T(8,128)} %bitcast.5) | data formatting | bytes 36864 | tf_op jit(solution)/shard_map/transpose | solution.py:624
  77.2 0.0 copy-start
  77.2 0.8 %reshape.18 = f32[4,1152]{1,0:T(4,128)} reshape(f32[4,128,9]{2,1,0:T(8,128)S(1)} %copy.5) | data formatting | bytes 36864 | tf_op jit(solution)/shard_map/reshape | solution.py:624
  78.1 0.0 copy-done
  78.1 0.5 copy.7
Async XLA Ops:
  77.2 0.8 %copy-start = (f32[1,16]{1,0:T(1,128)S(1)}, f32[1,16]{1,0:T(1,128)}, u32[]{:S(2)}) copy-start(f32[1,16]{1,0:T(1,128)} %get-tuple-element.5) | copy-start | bytes 196

commit v4 on v3

--- a/solution.py
+++ b/solution.py
@@ -363,8 +363,8 @@
         gram_piece(i)
     send_part(1)
     reduce_plane(0)
+    spread_sum(0)
     reduce_plane(1)
-    spread_sum(0)
     spread_sum(1)
     gathered(0)
     complete(0)

time: 78.8 us -> 75.6 us (0.959)
  Pallas kernels: 75.7 us -> 72.6 us
    pallas_call x1, Pallas kernels: 75.7 us -> 72.6 us  [whole(): pl.pallas_call(whole_kernel, out_shape=(jax.ShapeDtypeStruct((OUT_OWN, OF...]
where the time goes in v4:
time: 75.6 us; the launch traced here: 75.4 us
  Pallas kernels  72.6 us (96%)
  local copies, waits for them, and re-layouts  2.22 us (3%)
    pallas_call x1, Pallas kernels, whole(): pl.pallas_call(whole_kernel, out_shape=(jax.ShapeDtypeStruct((OUT_OWN, OF...  72.6 us

profile of v4, /device:TPU:1, one launch (start us, length us, event | category | flops | bytes accessed | tf_op | source)
XLA Modules:
  0.0 75.4 jit_solution(14829822165522534571)
XLA Ops:
  0.6 72.6 %shard_map.50 = (f32[4,9,128]{2,1,0:T(8,128)}, f32[1,16]{1,0:T(1,128)}) custom-call(bf16[16,128,256]{2,1,0:T(8,128)(2,1)} %bitcast.4, bf16[16,2,4,256]{3,2,1,0:T(4,128)(2,1)} %cot_hbm.1, f32[1,16]{1,0:T(1,128)} %bitcast.6), custom_call_target="tpu_custom_call" | custom-call | tf_op jit(solution)/shard_map/pallas_call | solution.py:454
  73.2 0.9 %copy.5 = f32[4,128,9]{2,1,0:T(8,128)S(1)} copy(f32[4,128,9]{1,2,0:T(8,128)} %bitcast.5) | data formatting | bytes 36864 | tf_op jit(solution)/shard_map/transpose | solution.py:624
  74.1 0.0 copy-start
  74.1 0.8 %reshape.18 = f32[4,1152]{1,0:T(4,128)} reshape(f32[4,128,9]{2,1,0:T(8,128)S(1)} %copy.5) | data formatting | bytes 36864 | tf_op jit(solution)/shard_map/reshape | solution.py:624
  74.9 0.0 copy-done
  74.9 0.5 copy.7
Async XLA Ops:
  74.1 0.8 %copy-start = (f32[1,16]{1,0:T(1,128)S(1)}, f32[1,16]{1,0:T(1,128)}, u32[]{:S(2)}) copy-start(f32[1,16]{1,0:T(1,128)} %get-tuple-element.5) | copy-start | bytes 196

commit v5 on v4

--- a/solution.py
+++ b/solution.py
@@ -274,7 +274,7 @@
     pl.semaphore_wait(ready, N_Y - 1)
 
     def place(at_z, at_y):
-        return ((at_z * N_Y + at_y) * 13) % PLANE
+        return ((at_z * N_Y + at_y) * 13 + core * (PLANE // 2)) % PLANE
 
     me = place(z, y)
 

time: 75.6 us -> 74.4 us (0.984)
  Pallas kernels: 72.6 us -> 71.4 us
    pallas_call x1, Pallas kernels: 72.6 us -> 71.4 us  [whole(): pl.pallas_call(whole_kernel, out_shape=(jax.ShapeDtypeStruct((OUT_OWN, OF...]
where the time goes in v5:
time: 74.4 us; the launch traced here: 74.2 us
  Pallas kernels  71.4 us (96%)
  local copies, waits for them, and re-layouts  2.22 us (3%)
    pallas_call x1, Pallas kernels, whole(): pl.pallas_call(whole_kernel, out_shape=(jax.ShapeDtypeStruct((OUT_OWN, OF...  71.4 us

profile of v5, /device:TPU:1, one launch (start us, length us, event | category | flops | bytes accessed | tf_op | source)
XLA Modules:
  0.0 74.2 jit_solution(6787694257142539456)
XLA Ops:
  0.6 71.4 %shard_map.50 = (f32[4,9,128]{2,1,0:T(8,128)}, f32[1,16]{1,0:T(1,128)}) custom-call(bf16[16,128,256]{2,1,0:T(8,128)(2,1)} %bitcast.4, bf16[16,2,4,256]{3,2,1,0:T(4,128)(2,1)} %cot_hbm.1, f32[1,16]{1,0:T(1,128)} %bitcast.6), custom_call_target="tpu_custom_call" | custom-call | tf_op jit(solution)/shard_map/pallas_call | solution.py:454
  72.0 0.9 %copy.5 = f32[4,128,9]{2,1,0:T(8,128)S(1)} copy(f32[4,128,9]{1,2,0:T(8,128)} %bitcast.5) | data formatting | bytes 36864 | tf_op jit(solution)/shard_map/transpose | solution.py:624
  72.9 0.0 copy-start
  72.9 0.8 %reshape.18 = f32[4,1152]{1,0:T(4,128)} reshape(f32[4,128,9]{2,1,0:T(8,128)S(1)} %copy.5) | data formatting | bytes 36864 | tf_op jit(solution)/shard_map/reshape | solution.py:624
  73.7 0.0 copy-done
  73.7 0.5 copy.7
Async XLA Ops:
  72.9 0.8 %copy-start = (f32[1,16]{1,0:T(1,128)S(1)}, f32[1,16]{1,0:T(1,128)}, u32[]{:S(2)}) copy-start(f32[1,16]{1,0:T(1,128)} %get-tuple-element.5) | copy-start | bytes 196
